TPU v7x, 512 devices: a whole 4x8x8 slice. The times are simulated.
512 devices in a mesh: ctx: 32 (over z, y_hi, core), tp: 16 (over x, y_lo).
Axes of the slice: x: 4, y: 8 (y_hi: 2, y_lo: 4; y = y_hi * 4 + y_lo), z: 8, core: 2. Of those that a mesh axis runs over, the one named last changes fastest.
Arguments:
- q_proj: bfloat16 [4096, 4096], P('ctx', 'tp'), may hold values from -6 to 6
- k_proj: bfloat16 [4096, 4096], P('ctx', 'tp'), may hold values from -6 to 6
- v_proj: bfloat16 [4096, 4096], P('ctx', 'tp'), may hold values from -6 to 6
- saved_conv: bfloat16 [4096, 4096], P('ctx', 'tp'), may hold values from -6 to 6
- out_grad: bfloat16 [4096, 4096], P('ctx', 'tp'), may hold values from -6 to 6
- out_weight: bfloat16 [4096, 4096], P('tp'), may hold values from -0.09375 to 0.09375
- filter_taps: bfloat16 [4096, 4096], P('ctx', 'tp'), may hold values from -1.1 to 1.1
Outputs:
- dq_grad: bfloat16 [4096, 4096], P('ctx', 'tp')
- dk_grad: bfloat16 [4096, 4096], P('ctx', 'tp')
- dv_grad: bfloat16 [4096, 4096], P('ctx', 'tp')
- filter_grad: float32 [4096, 4096], P('ctx', 'tp')
All inputs are finite; a program needn't handle non-finite values.
Results may differ from a plain program's by a relative error of at most 0.003.
Values may be sent and summed in bfloat16 or wider, within the bound.
A program may use at most 128 MiB of HBM per device.

v0:
```python
import math
import jax
import jax.numpy as jnp
from jax import lax
from jax.sharding import PartitionSpec as P


def from_behind(value, axis, steps):
    count = lax.axis_size(axis)
    pairs = [(source, (source + steps) % count) for source in range(count)]
    return lax.ppermute(value, axis, pairs)


def passed_along(block, axis, distance):
    devices = range(lax.axis_size(axis))
    route = [(i - distance, i) for i in devices if i - distance in devices]
    return lax.ppermute(block, axis, route)


def matmul(left, right):
    return jnp.dot(left, right, precision=lax.Precision.HIGHEST, preferred_element_type=jnp.float32)


def split_table(table):
    upper = lax.optimization_barrier(table.astype(jnp.bfloat16))
    lower = (table - upper.astype(jnp.float32)).astype(jnp.bfloat16)
    return (upper, lower)


def half_matmul(table, signal):
    upper, lower = split_table(table)
    return jnp.dot(upper, signal, preferred_element_type=jnp.float32) + jnp.dot(
        lower, signal, preferred_element_type=jnp.float32
    )


def make_tables(rows):
    index = jnp.arange(rows, dtype=jnp.int32)
    long_index = jnp.arange(2 * rows, dtype=jnp.int32)
    angle = (index[:, None] * index[None, :] % (2 * rows)).astype(jnp.float32) * (math.pi / rows)
    angle_back = (long_index[:, None] * index[None, :] % (2 * rows)).astype(jnp.float32) * (
        math.pi / rows
    )
    weight = jnp.where(index == 0, 1.0, 2.0).astype(jnp.float32) / (2.0 * rows)
    alternate = (1 - 2 * (index % 2)).astype(jnp.float32)
    alternate_back = (1 - 2 * (long_index % 2)).astype(jnp.float32) / (2.0 * rows)
    return (
        jnp.cos(angle),
        -jnp.sin(angle),
        alternate,
        jnp.cos(angle_back) * weight[None, :],
        -jnp.sin(angle_back) * weight[None, :],
        alternate_back,
    )


def forward(signal, tables):
    fwd_cos, fwd_sin, alternate = (tables[0], tables[1], tables[2])
    return (matmul(fwd_cos, signal), matmul(fwd_sin, signal), matmul(alternate[None, :], signal))


def forward_half(signal, tables):
    fwd_cos, fwd_sin, alternate = (tables[0], tables[1], tables[2])
    signs = alternate[None, :].astype(jnp.bfloat16)
    return (
        half_matmul(fwd_cos, signal),
        half_matmul(fwd_sin, signal),
        jnp.dot(signs, signal, preferred_element_type=jnp.float32),
    )


def inverse(spectrum, tables, count):
    inv_cos, inv_sin, alternate_back = (tables[3], tables[4], tables[5])
    return (
        matmul(inv_cos[:count], spectrum[0])
        + matmul(inv_sin[:count], spectrum[1])
        + alternate_back[:count, None] * spectrum[2]
    )


def correlate(first, second):
    real_part = first[0] * second[0] + first[1] * second[1]
    imag_part = first[0] * second[1] - first[1] * second[0]
    return (real_part, imag_part, first[2] * second[2])


def add_lags(filter_terms, lagged, step, active, rows):
    later = jnp.asarray(step >= 1, jnp.float32)
    filter_terms = filter_terms.at[step].add(lagged[:rows] * active)
    return filter_terms.at[jnp.maximum(step - 1, 0)].add(lagged[rows:] * (active * later))


def body(q_proj, k_proj, v_proj, saved_conv, out_grad, out_weight, filter_taps):
    rows = q_proj.shape[0]
    chans = q_proj.shape[1]
    blocks = lax.axis_size("ctx")
    me_index = lax.axis_index("ctx")
    tables = make_tables(rows)
    empty = jnp.zeros((rows, chans), jnp.float32)
    d_gated = lax.dot_general(
        lax.all_gather(out_grad, "tp", axis=1, tiled=True),
        out_weight,
        (((1,), (1,)), ((), ())),
        preferred_element_type=jnp.float32,
    )
    dq_grad = (d_gated * saved_conv.astype(jnp.float32)).astype(jnp.bfloat16)
    dz_local = d_gated * q_proj.astype(jnp.float32)
    gated = (k_proj.astype(jnp.float32) * v_proj.astype(jnp.float32)).astype(jnp.bfloat16)
    whole_filter = lax.all_gather(filter_taps, "ctx", axis=0, tiled=True)
    filter_blocks = whole_filter.reshape(blocks, rows, chans)
    cos_upper, cos_lower = split_table(tables[0])
    sin_upper, sin_lower = split_table(tables[1])
    spec_real = jnp.einsum(
        "fn,bnc->bfc", cos_upper, filter_blocks, preferred_element_type=jnp.float32
    ) + jnp.einsum("fn,bnc->bfc", cos_lower, filter_blocks, preferred_element_type=jnp.float32)
    spec_imag = jnp.einsum(
        "fn,bnc->bfc", sin_upper, filter_blocks, preferred_element_type=jnp.float32
    ) + jnp.einsum("fn,bnc->bfc", sin_lower, filter_blocks, preferred_element_type=jnp.float32)
    spec_top = jnp.einsum(
        "n,bnc->bc",
        tables[2].astype(jnp.bfloat16),
        filter_blocks,
        preferred_element_type=jnp.float32,
    )[:, None, :]
    parity = tables[2][:, None]

    def lag_spectrum(step):
        earlier = jnp.maximum(step - 1, 0)
        keep = jnp.asarray(step >= 1, jnp.float32)
        pieces = []
        for stack, factor in ((spec_real, parity), (spec_imag, parity), (spec_top, 1.0)):
            current = lax.dynamic_index_in_dim(stack, step, 0, keepdims=False)
            before = lax.dynamic_index_in_dim(stack, earlier, 0, keepdims=False)
            pieces.append(current + keep * factor * before)
        return (pieces[0], pieces[1], pieces[2])

    filter_terms = jnp.zeros((blocks, rows, chans), jnp.float32)
    dz_spec = forward(dz_local, tables)

    def carried_step(step, state):
        partial_value, moving, terms = state
        active = jnp.asarray(me_index >= step, jnp.float32)
        partial_value = partial_value + active * inverse(
            correlate(lag_spectrum(step), dz_spec), tables, rows
        )
        moving_spec = forward_half(moving, tables)
        lagged = inverse(correlate(moving_spec, dz_spec), tables, 2 * rows)
        terms = add_lags(terms, lagged, step, active, rows)
        partial_value = from_behind(partial_value, "ctx", 1)
        moving = passed_along(moving, "ctx", 1)
        return (partial_value, moving, terms)

    du_local, moving_last, filter_terms = lax.fori_loop(
        0, blocks, carried_step, (empty, gated, filter_terms)
    )
    summed = lax.psum_scatter(
        filter_terms.reshape(blocks * rows, chans), "ctx", scatter_dimension=0, tiled=True
    )
    filter_grad = summed * float(rows * blocks) ** (-0.5)
    dk_grad = (du_local * v_proj.astype(jnp.float32)).astype(jnp.bfloat16)
    dv_grad = (du_local * k_proj.astype(jnp.float32)).astype(jnp.bfloat16)
    return (dq_grad, dk_grad, dv_grad, filter_grad)


def solution(mesh):
    in_specs = (
        P("ctx", "tp"),
        P("ctx", "tp"),
        P("ctx", "tp"),
        P("ctx", "tp"),
        P("ctx", "tp"),
        P("tp", None),
        P("ctx", "tp"),
    )
    out_specs = (P("ctx", "tp"), P("ctx", "tp"), P("ctx", "tp"), P("ctx", "tp"))
    return jax.shard_map(body, mesh=mesh, in_specs=in_specs, out_specs=out_specs, check_vma=False)
```

profile of v0, /device:TPU:2, one launch (start us, length us, event | category | flops | bytes accessed | tf_op | source)
XLA Modules:
  0.0 925.3 jit_solution(6137578330895444131)
XLA Ops:
  10.7 76.7 %all-gather.3.cloned.1.call-done = bf16[128,4096]{1,0:T(8,128)(2,1)} async-done(((bf16[128,256]{1,0:T(8,128)(2,1)}), bf16[128,4096]{1,0:T(8,128)(2,1)}) %all-gather.3.cloned.1.call-update) | async-done | bytes 1048592 | tf_op jit(solution)/shard_map/all_gather | solution.py:101
  92.2 89.1 %all-gather.5.cloned.1.call-done = bf16[4096,256]{1,0:T(8,128)(2,1)} async-done(((bf16[128,256]{1,0:T(8,128)(2,1)}), bf16[4096,256]{1,0:T(8,128)(2,1)}) %all-gather.5.cloned.1.call-update) | async-done | bytes 2097168 | tf_op jit(solution)/shard_map/all_gather | solution.py:109
  194.8 567.6 %while.23 = (s32[]{:T(128)}, f32[128,256]{0,1:T(8,128)S(1)}, bf16[128,256]{1,0:T(8,128)(2,1)S(1)}, f32[32,128,256]{1,2,0:T(8,128)}, s32[]{:T(128)}, /*index=5*/f...) while((s32[]{:T(128)}, f32[128,256]{0,1:T(8,128)S(1)}, ...), condition=%wide.region_3.4_spmd.clone.clone, body=%wide.region_0.3_spmd.clone.clone.sunk | while | flops 337464864 | bytes 7294348 | solution.py:153
  217.2 5.4 collective-permute-start
  252.2 5.7 collective-permute-start
  287.5 6.9 collective-permute-start
  324.1 5.4 collective-permute-start
  342.2 5.1 collective-permute-start
  359.8 5.4 collective-permute-start
  377.9 5.1 collective-permute-start
  395.4 5.1 collective-permute-start
  466.0 5.1 collective-permute-start
  484.4 5.1 collective-permute-start
  501.9 5.1 collective-permute-start
  537.0 5.1 collective-permute-start
  554.8 5.1 collective-permute-start
  608.8 5.1 collective-permute-start
  643.9 5.1 collective-permute-start
  679.5 5.1 collective-permute-start
  714.8 5.1 collective-permute-start
  732.5 5.1 collective-permute-start
  750.1 5.1 collective-permute-start
  762.4 5.6 copy.13
  769.6 147.7 %reduce-scatter.2.cloned.1.call-done = f32[128,256]{1,0:T(8,128)} async-done(((f32[4096,256]{1,0:T(8,128)}), f32[128,256]{1,0:T(8,128)}) %reduce-scatter.2.cloned.1.call-update) | async-done | bytes 131088 | tf_op jit(solution)/shard_map/reduce_scatter | solution.py:156
  (693 shorter events, 489.7 us)
Async XLA Ops:
  7.2 80.3 %all-gather.3.cloned.1.call-start = ((), (), s32[]{:S(2)}) async-start(), calls=%async_computation.1 | async-start | bytes 1114112 | tf_op jit(solution)/shard_map/all_gather | solution.py:101
  7.9 173.4 %all-gather.5.cloned.1.call-start = ((), (), s32[]{:S(2)}) async-start(), calls=%async_computation.2 | async-start | bytes 2162688 | tf_op jit(solution)/shard_map/all_gather | solution.py:109
  8.7 908.6 %reduce-scatter.2.cloned.1.call-start = ((), (), s32[]{:S(2)}) async-start(), calls=%async_computation.3 | async-start | bytes 4325376 | tf_op jit(solution)/shard_map/reduce_scatter | solution.py:156
  247.6 17.6 %collective-permute-start.1 = (bf16[128,256]{1,0:T(8,128)(2,1)S(1)}, bf16[128,256]{1,0:T(8,128)(2,1)S(1)}, u32[]{:S(2)}, u32[]{:S(2)}) collective-permute-start(bf16[128,256]{1,0:T(8,128)(2,1)S(1)} %copy.25), channel_id=1, source_target_pairs={{0,16},{16,32},{32,48},{48,64},{64,80},{80,96},{96,112},{112,128},... | collective-permute-start | bytes 196616 | tf_op jit(solution)/shard_map/while/body/eval_jaxpr/ppermute | solution.py:17
  282.9 18.7 %collective-permute-start.1 = (bf16[128,256]{1,0:T(8,128)(2,1)S(1)}, bf16[128,256]{1,0:T(8,128)(2,1)S(1)}, u32[]{:S(2)}, u32[]{:S(2)}) collective-permute-start(bf16[128,256]{1,0:T(8,128)(2,1)S(1)} %copy.25), channel_id=1, source_target_pairs={{0,16},{16,32},{32,48},{48,64},{64,80},{80,96},{96,112},{112,128},... | collective-permute-start | bytes 196616 | tf_op jit(solution)/shard_map/while/body/eval_jaxpr/ppermute | solution.py:17
  336.7 17.8 %collective-permute-start.1 = (bf16[128,256]{1,0:T(8,128)(2,1)S(1)}, bf16[128,256]{1,0:T(8,128)(2,1)S(1)}, u32[]{:S(2)}, u32[]{:S(2)}) collective-permute-start(bf16[128,256]{1,0:T(8,128)(2,1)S(1)} %copy.25), channel_id=1, source_target_pairs={{0,16},{16,32},{32,48},{48,64},{64,80},{80,96},{96,112},{112,128},... | collective-permute-start | bytes 196616 | tf_op jit(solution)/shard_map/while/body/eval_jaxpr/ppermute | solution.py:17
  354.6 17.8 %collective-permute-start.1 = (bf16[128,256]{1,0:T(8,128)(2,1)S(1)}, bf16[128,256]{1,0:T(8,128)(2,1)S(1)}, u32[]{:S(2)}, u32[]{:S(2)}) collective-permute-start(bf16[128,256]{1,0:T(8,128)(2,1)S(1)} %copy.25), channel_id=1, source_target_pairs={{0,16},{16,32},{32,48},{48,64},{64,80},{80,96},{96,112},{112,128},... | collective-permute-start | bytes 196616 | tf_op jit(solution)/shard_map/while/body/eval_jaxpr/ppermute | solution.py:17
  372.4 17.8 %collective-permute-start.1 = (bf16[128,256]{1,0:T(8,128)(2,1)S(1)}, bf16[128,256]{1,0:T(8,128)(2,1)S(1)}, u32[]{:S(2)}, u32[]{:S(2)}) collective-permute-start(bf16[128,256]{1,0:T(8,128)(2,1)S(1)} %copy.25), channel_id=1, source_target_pairs={{0,16},{16,32},{32,48},{48,64},{64,80},{80,96},{96,112},{112,128},... | collective-permute-start | bytes 196616 | tf_op jit(solution)/shard_map/while/body/eval_jaxpr/ppermute | solution.py:17
  390.2 17.6 %collective-permute-start.1 = (bf16[128,256]{1,0:T(8,128)(2,1)S(1)}, bf16[128,256]{1,0:T(8,128)(2,1)S(1)}, u32[]{:S(2)}, u32[]{:S(2)}) collective-permute-start(bf16[128,256]{1,0:T(8,128)(2,1)S(1)} %copy.25), channel_id=1, source_target_pairs={{0,16},{16,32},{32,48},{48,64},{64,80},{80,96},{96,112},{112,128},... | collective-permute-start | bytes 196616 | tf_op jit(solution)/shard_map/while/body/eval_jaxpr/ppermute | solution.py:17
  407.8 17.7 %collective-permute-start.1 = (bf16[128,256]{1,0:T(8,128)(2,1)S(1)}, bf16[128,256]{1,0:T(8,128)(2,1)S(1)}, u32[]{:S(2)}, u32[]{:S(2)}) collective-permute-start(bf16[128,256]{1,0:T(8,128)(2,1)S(1)} %copy.25), channel_id=1, source_target_pairs={{0,16},{16,32},{32,48},{48,64},{64,80},{80,96},{96,112},{112,128},... | collective-permute-start | bytes 196616 | tf_op jit(solution)/shard_map/while/body/eval_jaxpr/ppermute | solution.py:17
  443.1 17.7 %collective-permute-start.1 = (bf16[128,256]{1,0:T(8,128)(2,1)S(1)}, bf16[128,256]{1,0:T(8,128)(2,1)S(1)}, u32[]{:S(2)}, u32[]{:S(2)}) collective-permute-start(bf16[128,256]{1,0:T(8,128)(2,1)S(1)} %copy.25), channel_id=1, source_target_pairs={{0,16},{16,32},{32,48},{48,64},{64,80},{80,96},{96,112},{112,128},... | collective-permute-start | bytes 196616 | tf_op jit(solution)/shard_map/while/body/eval_jaxpr/ppermute | solution.py:17
  460.8 17.5 %collective-permute-start.1 = (bf16[128,256]{1,0:T(8,128)(2,1)S(1)}, bf16[128,256]{1,0:T(8,128)(2,1)S(1)}, u32[]{:S(2)}, u32[]{:S(2)}) collective-permute-start(bf16[128,256]{1,0:T(8,128)(2,1)S(1)} %copy.25), channel_id=1, source_target_pairs={{0,16},{16,32},{32,48},{48,64},{64,80},{80,96},{96,112},{112,128},... | collective-permute-start | bytes 196616 | tf_op jit(solution)/shard_map/while/body/eval_jaxpr/ppermute | solution.py:17
  478.3 18.4 %collective-permute-start.1 = (bf16[128,256]{1,0:T(8,128)(2,1)S(1)}, bf16[128,256]{1,0:T(8,128)(2,1)S(1)}, u32[]{:S(2)}, u32[]{:S(2)}) collective-permute-start(bf16[128,256]{1,0:T(8,128)(2,1)S(1)} %copy.25), channel_id=1, source_target_pairs={{0,16},{16,32},{32,48},{48,64},{64,80},{80,96},{96,112},{112,128},... | collective-permute-start | bytes 196616 | tf_op jit(solution)/shard_map/while/body/eval_jaxpr/ppermute | solution.py:17
  496.7 17.5 %collective-permute-start.1 = (bf16[128,256]{1,0:T(8,128)(2,1)S(1)}, bf16[128,256]{1,0:T(8,128)(2,1)S(1)}, u32[]{:S(2)}, u32[]{:S(2)}) collective-permute-start(bf16[128,256]{1,0:T(8,128)(2,1)S(1)} %copy.25), channel_id=1, source_target_pairs={{0,16},{16,32},{32,48},{48,64},{64,80},{80,96},{96,112},{112,128},... | collective-permute-start | bytes 196616 | tf_op jit(solution)/shard_map/while/body/eval_jaxpr/ppermute | solution.py:17
  531.8 17.5 %collective-permute-start.1 = (bf16[128,256]{1,0:T(8,128)(2,1)S(1)}, bf16[128,256]{1,0:T(8,128)(2,1)S(1)}, u32[]{:S(2)}, u32[]{:S(2)}) collective-permute-start(bf16[128,256]{1,0:T(8,128)(2,1)S(1)} %copy.25), channel_id=1, source_target_pairs={{0,16},{16,32},{32,48},{48,64},{64,80},{80,96},{96,112},{112,128},... | collective-permute-start | bytes 196616 | tf_op jit(solution)/shard_map/while/body/eval_jaxpr/ppermute | solution.py:17
  549.3 17.8 %collective-permute-start.1 = (bf16[128,256]{1,0:T(8,128)(2,1)S(1)}, bf16[128,256]{1,0:T(8,128)(2,1)S(1)}, u32[]{:S(2)}, u32[]{:S(2)}) collective-permute-start(bf16[128,256]{1,0:T(8,128)(2,1)S(1)} %copy.25), channel_id=1, source_target_pairs={{0,16},{16,32},{32,48},{48,64},{64,80},{80,96},{96,112},{112,128},... | collective-permute-start | bytes 196616 | tf_op jit(solution)/shard_map/while/body/eval_jaxpr/ppermute | solution.py:17
  567.1 17.5 %collective-permute-start.1 = (bf16[128,256]{1,0:T(8,128)(2,1)S(1)}, bf16[128,256]{1,0:T(8,128)(2,1)S(1)}, u32[]{:S(2)}, u32[]{:S(2)}) collective-permute-start(bf16[128,256]{1,0:T(8,128)(2,1)S(1)} %copy.25), channel_id=1, source_target_pairs={{0,16},{16,32},{32,48},{48,64},{64,80},{80,96},{96,112},{112,128},... | collective-permute-start | bytes 196616 | tf_op jit(solution)/shard_map/while/body/eval_jaxpr/ppermute | solution.py:17
  584.6 18.9 %collective-permute-start.1 = (bf16[128,256]{1,0:T(8,128)(2,1)S(1)}, bf16[128,256]{1,0:T(8,128)(2,1)S(1)}, u32[]{:S(2)}, u32[]{:S(2)}) collective-permute-start(bf16[128,256]{1,0:T(8,128)(2,1)S(1)} %copy.25), channel_id=1, source_target_pairs={{0,16},{16,32},{32,48},{48,64},{64,80},{80,96},{96,112},{112,128},... | collective-permute-start | bytes 196616 | tf_op jit(solution)/shard_map/while/body/eval_jaxpr/ppermute | solution.py:17
  621.1 17.5 %collective-permute-start.1 = (bf16[128,256]{1,0:T(8,128)(2,1)S(1)}, bf16[128,256]{1,0:T(8,128)(2,1)S(1)}, u32[]{:S(2)}, u32[]{:S(2)}) collective-permute-start(bf16[128,256]{1,0:T(8,128)(2,1)S(1)} %copy.25), channel_id=1, source_target_pairs={{0,16},{16,32},{32,48},{48,64},{64,80},{80,96},{96,112},{112,128},... | collective-permute-start | bytes 196616 | tf_op jit(solution)/shard_map/while/body/eval_jaxpr/ppermute | solution.py:17
  638.6 17.5 %collective-permute-start.1 = (bf16[128,256]{1,0:T(8,128)(2,1)S(1)}, bf16[128,256]{1,0:T(8,128)(2,1)S(1)}, u32[]{:S(2)}, u32[]{:S(2)}) collective-permute-start(bf16[128,256]{1,0:T(8,128)(2,1)S(1)} %copy.25), channel_id=1, source_target_pairs={{0,16},{16,32},{32,48},{48,64},{64,80},{80,96},{96,112},{112,128},... | collective-permute-start | bytes 196616 | tf_op jit(solution)/shard_map/while/body/eval_jaxpr/ppermute | solution.py:17
  656.2 18.0 %collective-permute-start.1 = (bf16[128,256]{1,0:T(8,128)(2,1)S(1)}, bf16[128,256]{1,0:T(8,128)(2,1)S(1)}, u32[]{:S(2)}, u32[]{:S(2)}) collective-permute-start(bf16[128,256]{1,0:T(8,128)(2,1)S(1)} %copy.25), channel_id=1, source_target_pairs={{0,16},{16,32},{32,48},{48,64},{64,80},{80,96},{96,112},{112,128},... | collective-permute-start | bytes 196616 | tf_op jit(solution)/shard_map/while/body/eval_jaxpr/ppermute | solution.py:17
  691.8 17.8 %collective-permute-start.1 = (bf16[128,256]{1,0:T(8,128)(2,1)S(1)}, bf16[128,256]{1,0:T(8,128)(2,1)S(1)}, u32[]{:S(2)}, u32[]{:S(2)}) collective-permute-start(bf16[128,256]{1,0:T(8,128)(2,1)S(1)} %copy.25), channel_id=1, source_target_pairs={{0,16},{16,32},{32,48},{48,64},{64,80},{80,96},{96,112},{112,128},... | collective-permute-start | bytes 196616 | tf_op jit(solution)/shard_map/while/body/eval_jaxpr/ppermute | solution.py:17
  727.1 17.7 %collective-permute-start.1 = (bf16[128,256]{1,0:T(8,128)(2,1)S(1)}, bf16[128,256]{1,0:T(8,128)(2,1)S(1)}, u32[]{:S(2)}, u32[]{:S(2)}) collective-permute-start(bf16[128,256]{1,0:T(8,128)(2,1)S(1)} %copy.25), channel_id=1, source_target_pairs={{0,16},{16,32},{32,48},{48,64},{64,80},{80,96},{96,112},{112,128},... | collective-permute-start | bytes 196616 | tf_op jit(solution)/shard_map/while/body/eval_jaxpr/ppermute | solution.py:17
  744.9 17.5 %collective-permute-start.1 = (bf16[128,256]{1,0:T(8,128)(2,1)S(1)}, bf16[128,256]{1,0:T(8,128)(2,1)S(1)}, u32[]{:S(2)}, u32[]{:S(2)}) collective-permute-start(bf16[128,256]{1,0:T(8,128)(2,1)S(1)} %copy.25), channel_id=1, source_target_pairs={{0,16},{16,32},{32,48},{48,64},{64,80},{80,96},{96,112},{112,128},... | collective-permute-start | bytes 196616 | tf_op jit(solution)/shard_map/while/body/eval_jaxpr/ppermute | solution.py:17
  (49 other events, 756.6 us)
Sparse Core Ops, SparseCore 0:
  10.0 77.3 all-gather.2
  90.8 90.4 all-gather.4
  768.2 149.0 reduce-scatter.1
where the time goes:
time: 931 us; the launch traced here: 925 us
  waiting for transfers between devices  322 us (35%)
  starting transfers between devices  223 us (24%)
  matrix products  181 us (19%)
  other arithmetic  173 us (19%)
  between operations  13.8 us (1%)
    ppermute x32, starting transfers between devices, from_behind(): return lax.ppermute(value, axis, pairs)  159 us
    reduce_scatter x1, waiting for transfers between devices, body(): lax.psum_scatter(filter_terms.reshape(blocks * rows, chans), 'ctx', scatt...  148 us
    dot_general x131, matrix products, matmul(): jnp.dot(left, right, precision=lax.Precision.HIGHEST, preferred_element_t...  129 us
    all_gather x1, waiting for transfers between devices, body(): whole_filter = lax.all_gather(filter_taps, 'ctx', axis=0, tiled=True)  89.1 us
    all_gather x1, waiting for transfers between devices, body(): lax.all_gather(out_grad, 'tp', axis=1, tiled=True)  76.7 us
    scatter-add x32, other arithmetic, add_lags(): filter_terms = filter_terms.at[step].add(lagged[:rows] * active)  72.8 us
    scatter-add x32, other arithmetic, add_lags(): filter_terms.at[jnp.maximum(step - 1, 0)]  70 us
    ppermute x32, starting transfers between devices, passed_along(): return lax.ppermute(block, axis, route)  64.1 us
  transfers between devices with their start and end apart: 67, of which 8 were waited for; matrix products, arithmetic and copies ran while one was open for 37% of the time, Pallas kernels for 0%

commit v1 on v0

--- a/solution.py
+++ b/solution.py
@@ -3,6 +3,13 @@
 import jax.numpy as jnp
 from jax import lax
 from jax.sharding import PartitionSpec as P
+
+
+def gather_over(x, axis, d):
+    size = lax.axis_size(axis)
+    parts = jnp.stack([x for _ in range(size)])
+    parts = lax.all_to_all(parts, axis, split_axis=0, concat_axis=0)
+    return jnp.concatenate(parts, axis=d)
 
 
 def from_behind(value, axis, steps):
@@ -106,7 +113,7 @@
     dq_grad = (d_gated * saved_conv.astype(jnp.float32)).astype(jnp.bfloat16)
     dz_local = d_gated * q_proj.astype(jnp.float32)
     gated = (k_proj.astype(jnp.float32) * v_proj.astype(jnp.float32)).astype(jnp.bfloat16)
-    whole_filter = lax.all_gather(filter_taps, "ctx", axis=0, tiled=True)
+    whole_filter = gather_over(filter_taps, "ctx", 0)
     filter_blocks = whole_filter.reshape(blocks, rows, chans)
     cos_upper, cos_lower = split_table(tables[0])
     sin_upper, sin_lower = split_table(tables[1])

time: 931 us -> 893 us (0.959)
  waiting for transfers between devices: 322 us -> 252 us
  starting transfers between devices: 223 us -> 254 us
    all_gather x1 -> x0, waiting for transfers between devices: 89.1 us -> none  [body(): whole_filter = lax.all_gather(filter_taps, 'ctx', axis=0, tiled=True)]
    ppermute x32, starting transfers between devices: 159 us -> 179 us  [from_behind(): return lax.ppermute(value, axis, pairs)]
    all_gather x1, waiting for transfers between devices: 76.7 us -> 96.2 us  [body(): lax.all_gather(out_grad, 'tp', axis=1, tiled=True)]
    all_to_all x0 -> x1, starting transfers between devices: none -> 16.2 us  [gather_over(): parts = lax.all_to_all(parts, axis, split_axis=0, concat_axis=0)]
  transfers between devices with their start and end apart: 67 -> 67, of which waited for: 8 -> 7; matrix products, arithmetic and copies ran while one was open for 37% -> 38% of each run, Pallas kernels for 0% -> 0%
where the time goes in v1:
time: 893 us; the launch traced here: 887 us
  starting transfers between devices  254 us (28%)
  waiting for transfers between devices  252 us (28%)
  matrix products  185 us (21%)
  other arithmetic  168 us (19%)
  between operations  14.2 us (2%)
  local copies, waits for them, and re-layouts  11 us (1%)
    ppermute x32, starting transfers between devices, from_behind(): return lax.ppermute(value, axis, pairs)  179 us
    reduce_scatter x1, waiting for transfers between devices, body(): lax.psum_scatter(filter_terms.reshape(blocks * rows, chans), 'ctx', scatt...  147 us
    dot_general x131, matrix products, matmul(): jnp.dot(left, right, precision=lax.Precision.HIGHEST, preferred_element_t...  128 us
    all_gather x1, waiting for transfers between devices, body(): lax.all_gather(out_grad, 'tp', axis=1, tiled=True)  96.2 us
    scatter-add x32, other arithmetic, add_lags(): filter_terms.at[jnp.maximum(step - 1, 0)]  70.2 us
    scatter-add x32, other arithmetic, add_lags(): filter_terms = filter_terms.at[step].add(lagged[:rows] * active)  69.8 us
    ppermute x32, starting transfers between devices, passed_along(): return lax.ppermute(block, axis, route)  59 us
    dot_general x64, matrix products, half_matmul(): jnp.dot(lower, signal, preferred_element_type=jnp.float32)  25.2 us
  transfers between devices with their start and end apart: 67, of which 7 were waited for; matrix products, arithmetic and copies ran while one was open for 38% of the time, Pallas kernels for 0%

profile of v1, /device:TPU:2, one launch (start us, length us, event | category | flops | bytes accessed | tf_op | source)
XLA Modules:
  0.0 887.4 jit_solution(7281938196282652542)
XLA Ops:
  9.8 16.2 %all-to-all-start = ((bf16[32,128,256]{2,1,0:T(8,128)(2,1)}), bf16[32,128,256]{2,1,0:T(8,128)(2,1)}, u32[]{:S(2)}, u32[]{:S(2)}) async-start(bf16[32,128,256]{2,1,0:T(8,128)(2,1)} %stack.2), calls=%async_computation | async-start | bytes 4194304 | tf_op jit(solution)/shard_map/all_to_all | solution.py:11
  27.9 96.2 %all-gather.2.cloned.1.call-done = bf16[128,4096]{1,0:T(8,128)(2,1)} async-done(((bf16[128,256]{1,0:T(8,128)(2,1)}), bf16[128,4096]{1,0:T(8,128)(2,1)}) %all-gather.2.cloned.1.call-update) | async-done | bytes 1048592 | tf_op jit(solution)/shard_map/all_gather | solution.py:108
  146.2 579.5 %while.23 = (s32[]{:T(128)}, f32[128,256]{0,1:T(8,128)S(1)}, bf16[128,256]{1,0:T(8,128)(2,1)S(1)}, f32[32,128,256]{1,2,0:T(8,128)}, s32[]{:T(128)}, /*index=5*/f...) while((s32[]{:T(128)}, f32[128,256]{0,1:T(8,128)S(1)}, ...), condition=%wide.region_3.4_spmd.clone.clone, body=%wide.region_0.3_spmd.clone.clone.sunk | while | flops 337464864 | bytes 7294348 | solution.py:160
  150.8 6.4 collective-permute-start
  204.9 6.2 collective-permute-start
  223.5 7.9 collective-permute-start
  243.7 5.4 collective-permute-start
  279.3 16.1 %collective-permute-start = (f32[128,256]{0,1:T(8,128)S(1)}, f32[128,256]{0,1:T(8,128)S(1)}, u32[]{:S(2)}, u32[]{:S(2)}) collective-permute-start(f32[128,256]{0,1:T(8,128)S(1)} %fusion.225), channel_id=1, source_target_pairs={{0,16},{16,32},{32,48},{48,64},{64,80},{80,96},{96,112},{112,128},... | collective-permute-start | bytes 393224 | tf_op jit(solution)/shard_map/while/body/eval_jaxpr/ppermute | solution.py:18
  307.8 5.3 collective-permute-start
  325.4 6.1 collective-permute-start
  343.8 5.3 collective-permute-start
  361.5 5.2 collective-permute-start
  431.6 5.2 collective-permute-start
  484.1 5.2 collective-permute-start
  501.7 5.2 collective-permute-start
  571.8 5.2 collective-permute-start
  589.5 5.2 collective-permute-start
  607.1 5.2 collective-permute-start
  625.5 5.3 collective-permute-start
  643.2 5.2 collective-permute-start
  660.7 5.2 collective-permute-start
  678.3 5.2 collective-permute-start
  725.7 5.6 copy.13
  732.1 146.9 %reduce-scatter.2.cloned.1.call-done = f32[128,256]{1,0:T(8,128)} async-done(((f32[4096,256]{1,0:T(8,128)}), f32[128,256]{1,0:T(8,128)}) %reduce-scatter.2.cloned.1.call-update) | async-done | bytes 131088 | tf_op jit(solution)/shard_map/reduce_scatter | solution.py:163
  (693 shorter events, 489.3 us)
Async XLA Ops:
  9.8 118.3 %all-to-all-start = ((bf16[32,128,256]{2,1,0:T(8,128)(2,1)}), bf16[32,128,256]{2,1,0:T(8,128)(2,1)}, u32[]{:S(2)}, u32[]{:S(2)}) async-start(bf16[32,128,256]{2,1,0:T(8,128)(2,1)} %stack.2), calls=%async_computation | async-start | bytes 4194304 | tf_op jit(solution)/shard_map/all_to_all | solution.py:11
  26.0 98.1 %all-gather.2.cloned.1.call-start = ((), (), s32[]{:S(2)}) async-start(), calls=%async_computation.2 | async-start | bytes 1114112 | tf_op jit(solution)/shard_map/all_gather | solution.py:108
  26.7 852.3 %reduce-scatter.2.cloned.1.call-start = ((), (), s32[]{:S(2)}) async-start(), calls=%async_computation.3 | async-start | bytes 4325376 | tf_op jit(solution)/shard_map/reduce_scatter | solution.py:163
  146.2 18.1 %collective-permute-start.1 = (bf16[128,256]{1,0:T(8,128)(2,1)S(1)}, bf16[128,256]{1,0:T(8,128)(2,1)S(1)}, u32[]{:S(2)}, u32[]{:S(2)}) collective-permute-start(bf16[128,256]{1,0:T(8,128)(2,1)S(1)} %copy.25), channel_id=1, source_target_pairs={{0,16},{16,32},{32,48},{48,64},{64,80},{80,96},{96,112},{112,128},... | collective-permute-start | bytes 196616 | tf_op jit(solution)/shard_map/while/body/eval_jaxpr/ppermute | solution.py:24
  200.3 17.9 %collective-permute-start.1 = (bf16[128,256]{1,0:T(8,128)(2,1)S(1)}, bf16[128,256]{1,0:T(8,128)(2,1)S(1)}, u32[]{:S(2)}, u32[]{:S(2)}) collective-permute-start(bf16[128,256]{1,0:T(8,128)(2,1)S(1)} %copy.25), channel_id=1, source_target_pairs={{0,16},{16,32},{32,48},{48,64},{64,80},{80,96},{96,112},{112,128},... | collective-permute-start | bytes 196616 | tf_op jit(solution)/shard_map/while/body/eval_jaxpr/ppermute | solution.py:24
  218.2 20.2 %collective-permute-start.1 = (bf16[128,256]{1,0:T(8,128)(2,1)S(1)}, bf16[128,256]{1,0:T(8,128)(2,1)S(1)}, u32[]{:S(2)}, u32[]{:S(2)}) collective-permute-start(bf16[128,256]{1,0:T(8,128)(2,1)S(1)} %copy.25), channel_id=1, source_target_pairs={{0,16},{16,32},{32,48},{48,64},{64,80},{80,96},{96,112},{112,128},... | collective-permute-start | bytes 196616 | tf_op jit(solution)/shard_map/while/body/eval_jaxpr/ppermute | solution.py:24
  238.5 17.7 %collective-permute-start.1 = (bf16[128,256]{1,0:T(8,128)(2,1)S(1)}, bf16[128,256]{1,0:T(8,128)(2,1)S(1)}, u32[]{:S(2)}, u32[]{:S(2)}) collective-permute-start(bf16[128,256]{1,0:T(8,128)(2,1)S(1)} %copy.25), channel_id=1, source_target_pairs={{0,16},{16,32},{32,48},{48,64},{64,80},{80,96},{96,112},{112,128},... | collective-permute-start | bytes 196616 | tf_op jit(solution)/shard_map/while/body/eval_jaxpr/ppermute | solution.py:24
  274.7 27.8 %collective-permute-start.1 = (bf16[128,256]{1,0:T(8,128)(2,1)S(1)}, bf16[128,256]{1,0:T(8,128)(2,1)S(1)}, u32[]{:S(2)}, u32[]{:S(2)}) collective-permute-start(bf16[128,256]{1,0:T(8,128)(2,1)S(1)} %copy.25), channel_id=1, source_target_pairs={{0,16},{16,32},{32,48},{48,64},{64,80},{80,96},{96,112},{112,128},... | collective-permute-start | bytes 196616 | tf_op jit(solution)/shard_map/while/body/eval_jaxpr/ppermute | solution.py:24
  279.3 23.2 %collective-permute-start = (f32[128,256]{0,1:T(8,128)S(1)}, f32[128,256]{0,1:T(8,128)S(1)}, u32[]{:S(2)}, u32[]{:S(2)}) collective-permute-start(f32[128,256]{0,1:T(8,128)S(1)} %fusion.225), channel_id=1, source_target_pairs={{0,16},{16,32},{32,48},{48,64},{64,80},{80,96},{96,112},{112,128},... | collective-permute-start | bytes 393224 | tf_op jit(solution)/shard_map/while/body/eval_jaxpr/ppermute | solution.py:18
  302.5 17.6 %collective-permute-start.1 = (bf16[128,256]{1,0:T(8,128)(2,1)S(1)}, bf16[128,256]{1,0:T(8,128)(2,1)S(1)}, u32[]{:S(2)}, u32[]{:S(2)}) collective-permute-start(bf16[128,256]{1,0:T(8,128)(2,1)S(1)} %copy.25), channel_id=1, source_target_pairs={{0,16},{16,32},{32,48},{48,64},{64,80},{80,96},{96,112},{112,128},... | collective-permute-start | bytes 196616 | tf_op jit(solution)/shard_map/while/body/eval_jaxpr/ppermute | solution.py:24
  320.2 18.4 %collective-permute-start.1 = (bf16[128,256]{1,0:T(8,128)(2,1)S(1)}, bf16[128,256]{1,0:T(8,128)(2,1)S(1)}, u32[]{:S(2)}, u32[]{:S(2)}) collective-permute-start(bf16[128,256]{1,0:T(8,128)(2,1)S(1)} %copy.25), channel_id=1, source_target_pairs={{0,16},{16,32},{32,48},{48,64},{64,80},{80,96},{96,112},{112,128},... | collective-permute-start | bytes 196616 | tf_op jit(solution)/shard_map/while/body/eval_jaxpr/ppermute | solution.py:24
  356.2 17.5 %collective-permute-start.1 = (bf16[128,256]{1,0:T(8,128)(2,1)S(1)}, bf16[128,256]{1,0:T(8,128)(2,1)S(1)}, u32[]{:S(2)}, u32[]{:S(2)}) collective-permute-start(bf16[128,256]{1,0:T(8,128)(2,1)S(1)} %copy.25), channel_id=1, source_target_pairs={{0,16},{16,32},{32,48},{48,64},{64,80},{80,96},{96,112},{112,128},... | collective-permute-start | bytes 196616 | tf_op jit(solution)/shard_map/while/body/eval_jaxpr/ppermute | solution.py:24
  426.3 17.5 %collective-permute-start.1 = (bf16[128,256]{1,0:T(8,128)(2,1)S(1)}, bf16[128,256]{1,0:T(8,128)(2,1)S(1)}, u32[]{:S(2)}, u32[]{:S(2)}) collective-permute-start(bf16[128,256]{1,0:T(8,128)(2,1)S(1)} %copy.25), channel_id=1, source_target_pairs={{0,16},{16,32},{32,48},{48,64},{64,80},{80,96},{96,112},{112,128},... | collective-permute-start | bytes 196616 | tf_op jit(solution)/shard_map/while/body/eval_jaxpr/ppermute | solution.py:24
  443.9 17.5 %collective-permute-start.1 = (bf16[128,256]{1,0:T(8,128)(2,1)S(1)}, bf16[128,256]{1,0:T(8,128)(2,1)S(1)}, u32[]{:S(2)}, u32[]{:S(2)}) collective-permute-start(bf16[128,256]{1,0:T(8,128)(2,1)S(1)} %copy.25), channel_id=1, source_target_pairs={{0,16},{16,32},{32,48},{48,64},{64,80},{80,96},{96,112},{112,128},... | collective-permute-start | bytes 196616 | tf_op jit(solution)/shard_map/while/body/eval_jaxpr/ppermute | solution.py:24
  496.5 17.5 %collective-permute-start.1 = (bf16[128,256]{1,0:T(8,128)(2,1)S(1)}, bf16[128,256]{1,0:T(8,128)(2,1)S(1)}, u32[]{:S(2)}, u32[]{:S(2)}) collective-permute-start(bf16[128,256]{1,0:T(8,128)(2,1)S(1)} %copy.25), channel_id=1, source_target_pairs={{0,16},{16,32},{32,48},{48,64},{64,80},{80,96},{96,112},{112,128},... | collective-permute-start | bytes 196616 | tf_op jit(solution)/shard_map/while/body/eval_jaxpr/ppermute | solution.py:24
  566.6 17.5 %collective-permute-start.1 = (bf16[128,256]{1,0:T(8,128)(2,1)S(1)}, bf16[128,256]{1,0:T(8,128)(2,1)S(1)}, u32[]{:S(2)}, u32[]{:S(2)}) collective-permute-start(bf16[128,256]{1,0:T(8,128)(2,1)S(1)} %copy.25), channel_id=1, source_target_pairs={{0,16},{16,32},{32,48},{48,64},{64,80},{80,96},{96,112},{112,128},... | collective-permute-start | bytes 196616 | tf_op jit(solution)/shard_map/while/body/eval_jaxpr/ppermute | solution.py:24
  584.1 17.7 %collective-permute-start.1 = (bf16[128,256]{1,0:T(8,128)(2,1)S(1)}, bf16[128,256]{1,0:T(8,128)(2,1)S(1)}, u32[]{:S(2)}, u32[]{:S(2)}) collective-permute-start(bf16[128,256]{1,0:T(8,128)(2,1)S(1)} %copy.25), channel_id=1, source_target_pairs={{0,16},{16,32},{32,48},{48,64},{64,80},{80,96},{96,112},{112,128},... | collective-permute-start | bytes 196616 | tf_op jit(solution)/shard_map/while/body/eval_jaxpr/ppermute | solution.py:24
  601.9 17.6 %collective-permute-start.1 = (bf16[128,256]{1,0:T(8,128)(2,1)S(1)}, bf16[128,256]{1,0:T(8,128)(2,1)S(1)}, u32[]{:S(2)}, u32[]{:S(2)}) collective-permute-start(bf16[128,256]{1,0:T(8,128)(2,1)S(1)} %copy.25), channel_id=1, source_target_pairs={{0,16},{16,32},{32,48},{48,64},{64,80},{80,96},{96,112},{112,128},... | collective-permute-start | bytes 196616 | tf_op jit(solution)/shard_map/while/body/eval_jaxpr/ppermute | solution.py:24
  619.5 18.5 %collective-permute-start.1 = (bf16[128,256]{1,0:T(8,128)(2,1)S(1)}, bf16[128,256]{1,0:T(8,128)(2,1)S(1)}, u32[]{:S(2)}, u32[]{:S(2)}) collective-permute-start(bf16[128,256]{1,0:T(8,128)(2,1)S(1)} %copy.25), channel_id=1, source_target_pairs={{0,16},{16,32},{32,48},{48,64},{64,80},{80,96},{96,112},{112,128},... | collective-permute-start | bytes 196616 | tf_op jit(solution)/shard_map/while/body/eval_jaxpr/ppermute | solution.py:24
  637.9 17.5 %collective-permute-start.1 = (bf16[128,256]{1,0:T(8,128)(2,1)S(1)}, bf16[128,256]{1,0:T(8,128)(2,1)S(1)}, u32[]{:S(2)}, u32[]{:S(2)}) collective-permute-start(bf16[128,256]{1,0:T(8,128)(2,1)S(1)} %copy.25), channel_id=1, source_target_pairs={{0,16},{16,32},{32,48},{48,64},{64,80},{80,96},{96,112},{112,128},... | collective-permute-start | bytes 196616 | tf_op jit(solution)/shard_map/while/body/eval_jaxpr/ppermute | solution.py:24
  655.5 17.5 %collective-permute-start.1 = (bf16[128,256]{1,0:T(8,128)(2,1)S(1)}, bf16[128,256]{1,0:T(8,128)(2,1)S(1)}, u32[]{:S(2)}, u32[]{:S(2)}) collective-permute-start(bf16[128,256]{1,0:T(8,128)(2,1)S(1)} %copy.25), channel_id=1, source_target_pairs={{0,16},{16,32},{32,48},{48,64},{64,80},{80,96},{96,112},{112,128},... | collective-permute-start | bytes 196616 | tf_op jit(solution)/shard_map/while/body/eval_jaxpr/ppermute | solution.py:24
  673.0 17.5 %collective-permute-start.1 = (bf16[128,256]{1,0:T(8,128)(2,1)S(1)}, bf16[128,256]{1,0:T(8,128)(2,1)S(1)}, u32[]{:S(2)}, u32[]{:S(2)}) collective-permute-start(bf16[128,256]{1,0:T(8,128)(2,1)S(1)} %copy.25), channel_id=1, source_target_pairs={{0,16},{16,32},{32,48},{48,64},{64,80},{80,96},{96,112},{112,128},... | collective-permute-start | bytes 196616 | tf_op jit(solution)/shard_map/while/body/eval_jaxpr/ppermute | solution.py:24
  690.6 17.5 %collective-permute-start.1 = (bf16[128,256]{1,0:T(8,128)(2,1)S(1)}, bf16[128,256]{1,0:T(8,128)(2,1)S(1)}, u32[]{:S(2)}, u32[]{:S(2)}) collective-permute-start(bf16[128,256]{1,0:T(8,128)(2,1)S(1)} %copy.25), channel_id=1, source_target_pairs={{0,16},{16,32},{32,48},{48,64},{64,80},{80,96},{96,112},{112,128},... | collective-permute-start | bytes 196616 | tf_op jit(solution)/shard_map/while/body/eval_jaxpr/ppermute | solution.py:24
  708.1 17.5 %collective-permute-start.1 = (bf16[128,256]{1,0:T(8,128)(2,1)S(1)}, bf16[128,256]{1,0:T(8,128)(2,1)S(1)}, u32[]{:S(2)}, u32[]{:S(2)}) collective-permute-start(bf16[128,256]{1,0:T(8,128)(2,1)S(1)} %copy.25), channel_id=1, source_target_pairs={{0,16},{16,32},{32,48},{48,64},{64,80},{80,96},{96,112},{112,128},... | collective-permute-start | bytes 196616 | tf_op jit(solution)/shard_map/while/body/eval_jaxpr/ppermute | solution.py:24
  (49 other events, 988.8 us)
Sparse Core Ops, SparseCore 0:
  28.8 95.2 all-gather.1
  731.4 147.5 reduce-scatter.1
